TPU v7x, 256 devices: a whole 4x4x8 slice. The times are simulated.
256 devices in a mesh: sub: 64 (over x, z, core), layer: 4 (over y).
Axes of the slice: x: 4, y: 4, z: 8, core: 2. Of those that a mesh axis runs over, the one named last changes fastest.
Arguments:
- geometry: float32 [10, 4, 98304], P(None, 'layer', 'sub'), may hold values from -2 to 2, as said below
- dest_slot: int32 [4, 98304], P('layer', 'sub'), may hold values from 0 to 98303, as said below
- pairs: int32 [2, 4, 98304], P(None, 'layer', 'sub'), may hold values from 0 to 767, as said below
- colors: int32 [4, 768], P('layer', 'sub'), may hold values from 0 to 3
- free_vel: float32 [6, 4, 32768], P(None, 'layer', 'sub'), may hold values from -6 to 6
- inertia: float32 [4, 4, 32768], P(None, 'layer', 'sub'), may hold values from 0.5 to 3
- exports: int32 [4, 4, 4096], P(None, 'layer', 'sub'), may hold values from 0 to 511, as said below
Outputs:
- impulse: float32 [3, 4, 98304], P(None, 'layer', 'sub')
- velocity: float32 [6, 4, 32768], P(None, 'layer', 'sub')
Inputs may be any that keep to these rules, and one draw needn't show every extreme that they name: Within each layer dest_slot is a permutation of 0 to 98303; the owner of a detected contact lies in the same aligned group of 4 sub indices as the device that holds it. At most 768 contacts of one device go to one owner, and in every group some device hands exactly 768 to one owner. pairs[0] is an own block, 0 to 511. pairs[1] is another own block, or 512 + d * 64 + i, the copy of the i-th block that the neighbour in direction d (0 lower sub index, 1 higher, 2 lower layer, 3 higher layer) lists toward this subdomain; only directions with a neighbour appear. `exports`: each subdomain's list for one direction holds 64 distinct own blocks. `geometry`: rows 0 and 1 lie in -1 to 1 and row 2 in 0.5 to 1.5 (the normal before normalizing); rows 3 to 8 are lever arms, row 9 the gap rate within -1 to 1.
All inputs are finite; a program needn't handle non-finite values.
Results may differ from a plain program's by a relative error of at most 0.0003.
Values sent between devices are 32-bit elements; how exact they have to be, the bound alone decides.
A program may use at most 64 MiB of HBM per device.

v0:
```python
import jax
import jax.numpy as jnp
from jax import lax
from jax.experimental import pallas as pl
from jax.experimental.pallas import tpu as pltpu
from jax.sharding import PartitionSpec as P

WIN = 4
SWEEPS = 3
NCOLOR = 4
LANES = 128
TILES = 12
ROWS = 16
SPLIT = 256
OWN = 4
TABLE = 6

relaxation = 0.7
friction = 0.6
tangent_floor = 0.1

MESH = pl.DeviceIdType.MESH
F32 = jnp.float32
BF16 = jnp.bfloat16
NT = (((1,), (1,)), ((), ()))


def cross(u, v):
    return [
        u[1] * v[2] - u[2] * v[1],
        u[2] * v[0] - u[0] * v[2],
        u[0] * v[1] - u[1] * v[0],
    ]


def dot3(u, v):
    return u[0] * v[0] + u[1] * v[1] + u[2] * v[2]


def take(row_block, index):
    return jnp.take_along_axis(row_block, index, axis=1, mode="promise_in_bounds")


def coarse(value):
    return value.astype(BF16).astype(F32)


def arm_block(arm, spin):
    return [
        spin[1] * arm[2] * arm[2] + spin[2] * arm[1] * arm[1],
        spin[0] * arm[2] * arm[2] + spin[2] * arm[0] * arm[0],
        spin[0] * arm[1] * arm[1] + spin[1] * arm[0] * arm[0],
        -spin[2] * arm[0] * arm[1],
        -spin[1] * arm[0] * arm[2],
        -spin[0] * arm[1] * arm[2],
    ]


def kernel(
    n_sub,
    n_layer,
    geo_ref,
    slot_ref,
    pairs_ref,
    color_ref,
    free_ref,
    inertia_ref,
    exports_ref,
    imp_out,
    vel_out,
    slot_hot,
    pair_hot,
    split_geo,
    relay_left,
    push_left,
    outgoing,
    incoming,
    geo,
    index,
    shade,
    const,
    impulse,
    push,
    table,
    start,
    inverse_list,
    weight,
    first_out,
    first_in,
    round_out,
    round_in,
    relay_send,
    relay_recv,
    round_send,
    round_recv,
):
    sub = lax.axis_index("sub")
    layer = lax.axis_index("layer")
    base = (sub // WIN) * WIN
    place = sub - base
    lower_sub = lax.rem(sub + n_sub - 1, n_sub)
    higher_sub = lax.rem(sub + 1, n_sub)
    lower_layer = lax.rem(layer + n_layer - 1, n_layer)
    higher_layer = lax.rem(layer + 1, n_layer)

    def mate(step):
        return base + lax.rem(place + step, WIN)

    around = (
        ((lower_sub, layer), 1, 0),
        ((higher_sub, layer), 0, 0),
        ((sub, lower_layer), 3, 1),
        ((sub, higher_layer), 2, 1),
    )

    barrier = pltpu.get_barrier_semaphore()
    for device, _, _ in around:
        pl.semaphore_signal(barrier, inc=1, device_id=device, device_id_type=MESH)
    for step in range(1, WIN):
        pl.semaphore_signal(
            barrier, inc=1, device_id=(mate(step), layer), device_id_type=MESH
        )

    def trade(step, src, dst):
        return [
            pltpu.make_async_remote_copy(
                src_ref=src.at[pair],
                dst_ref=dst.at[slot],
                send_sem=round_send.at[step, slot],
                recv_sem=round_recv.at[step, slot],
                device_id=device,
                device_id_type=MESH,
            )
            for device, slot, pair in around
        ]

    def exchange(step):
        return trade(step, round_out.at[step - 1], round_in.at[step - 1])

    lane8 = lax.broadcasted_iota(jnp.int32, (8, LANES), 1)
    lane16 = lax.broadcasted_iota(jnp.int32, (ROWS, LANES), 1)

    table[...] = jnp.zeros_like(table)
    for h in range(OWN):
        cols = slice(h * LANES, (h + 1) * LANES)
        table[0:6, cols] = free_ref[pl.ds(h, 6, stride=OWN), :]
        table[8:12, cols] = inertia_ref[pl.ds(h, 4, stride=OWN), :]
    listed = [
        jnp.concatenate([exports_ref[1], exports_ref[0]], axis=1),
        jnp.concatenate([exports_ref[3], exports_ref[2]], axis=1),
    ]

    def pick_listed(pair, rows):
        high = jnp.broadcast_to(lax.shift_right_logical(listed[pair], 7), (rows, LANES))
        low = jnp.broadcast_to(lax.bitwise_and(listed[pair], 127), (rows, LANES))
        got = take(table[0:rows, 0:LANES], low)
        for h in range(1, OWN):
            block = take(table[0:rows, h * LANES : (h + 1) * LANES], low)
            got = jnp.where(high == h, block, got)
        return got

    for pair in range(2):
        first_out[pair] = pick_listed(pair, 16)

    for t in range(TILES):
        cols = slice(t * LANES, (t + 1) * LANES)
        main = geo_ref[pl.ds(t, 8, stride=TILES), :]
        rest = geo_ref[pl.ds(8 * TILES + t, 2, stride=TILES), :]
        main_a = coarse(main)
        main_b = coarse(main - main_a)
        rest_a = coarse(rest)
        rest_b = coarse(rest - rest_a)
        split_geo[0:8, cols] = main_a
        split_geo[8:16, cols] = main_b
        split_geo[16:24, cols] = main - main_a - main_b
        split_geo[24:26, cols] = rest_a
        split_geo[26:28, cols] = rest_b
        split_geo[28:30, cols] = rest - rest_a - rest_b
        split_geo[30:32, cols] = jnp.zeros((2, LANES), F32)

    spread = lax.broadcasted_iota(jnp.int32, (SPLIT, LANES), 0)
    for t in range(TILES):
        low = lax.bitwise_and(slot_ref[t : t + 1, :], SPLIT - 1)
        slot_hot[:, t * LANES : (t + 1) * LANES] = (spread == low).astype(F32).astype(BF16)

    pl.semaphore_wait(barrier, 7)
    first_trade = trade(0, first_out, first_in)
    for copy in first_trade:
        copy.start()

    def relay_copy(step):
        return pltpu.make_async_remote_copy(
            src_ref=outgoing.at[lax.rem(place + step, WIN)],
            dst_ref=incoming.at[step - 1],
            send_sem=relay_send.at[step - 1],
            recv_sem=relay_recv.at[step - 1],
            device_id=(mate(step), layer),
            device_id_type=MESH,
        )

    def arrange(target):
        for t in range(TILES):
            cols = slice(t * LANES, (t + 1) * LANES)
            part = lax.shift_right_logical(slot_ref[t : t + 1, :], 8)
            part = part - (base + target) * TABLE
            values = split_geo[:, cols]
            for g in range(TABLE):
                relay_left[g * 32 : (g + 1) * 32, cols] = jnp.where(
                    part == g, values, 0.0
                ).astype(BF16)
        placed = lax.dot_general(
            relay_left[...], slot_hot[...], NT, preferred_element_type=F32
        )
        for g in range(TABLE):
            block = placed[g * 32 : (g + 1) * 32]
            main = block[0:8] + block[8:16] + block[16:24]
            rest = block[24:26] + block[26:28] + block[28:30]
            for j in range(2):
                cols = slice(j * LANES, (j + 1) * LANES)
                t = 2 * g + j
                outgoing[target, pl.ds(t, 8, stride=TILES), :] = main[:, cols]
                outgoing[target, pl.ds(8 * TILES + t, 2, stride=TILES), :] = rest[:, cols]

    def send_part(step, carry):
        arrange(lax.rem(place + step, WIN))
        relay_copy(step).start()
        return carry

    lax.fori_loop(1, WIN, send_part, 0)
    arrange(place)

    index[...] = jnp.zeros_like(index)
    for e in range(2):
        index[e, 0:TILES] = pairs_ref[e * TILES : (e + 1) * TILES, :]
        for t in range(TILES):
            low = lax.bitwise_and(
                pairs_ref[e * TILES + t : e * TILES + t + 1, :], SPLIT - 1
            )
            at = (e * TILES + t) * LANES
            pair_hot[:, at : at + LANES] = (spread == low).astype(F32).astype(BF16)
    row16 = lax.broadcasted_iota(jnp.int32, (ROWS, LANES), 0)
    tint = jnp.full((ROWS, LANES), -1, jnp.int32)
    for t in range(TILES):
        tint = jnp.where(row16 == t, color_ref[0, t], tint)
    shade[...] = tint

    wide = lax.broadcasted_iota(jnp.int32, (16, 2 * LANES), 1)
    marks = jnp.where(
        lax.broadcasted_iota(jnp.int32, (16, 2 * LANES), 0) == wide // 64,
        lax.bitwise_and(wide, 127) + 1,
        0,
    )
    tall = lax.broadcasted_iota(jnp.int32, (OWN * LANES, LANES), 0)
    listed_hot = jnp.concatenate(
        [(tall == listed[pair]).astype(F32).astype(BF16) for pair in range(2)], axis=1
    )
    found = lax.dot_general(
        marks.astype(F32).astype(BF16), listed_hot, NT, preferred_element_type=F32
    )
    has_lower_sub = (sub > 0).astype(jnp.int32)
    has_higher_sub = (sub < n_sub - 1).astype(jnp.int32)
    has_lower_layer = (layer > 0).astype(jnp.int32)
    has_higher_layer = (layer < n_layer - 1).astype(jnp.int32)
    exists = (has_higher_sub, has_lower_sub, has_higher_layer, has_lower_layer)
    for h in range(OWN):
        cols = slice(h * LANES, (h + 1) * LANES)
        times = jnp.ones((8, LANES), F32)
        for half in range(4):
            spot = jnp.broadcast_to(found[half : half + 1, cols], (8, LANES))
            spot = spot.astype(jnp.int32) * exists[half] - 1
            inverse_list[h * 4 + half] = spot
            times = times + jnp.where(spot >= 0, 1.0, 0.0)
        weight[:, cols] = 1.0 / times
    push[...] = jnp.zeros_like(push)
    impulse[...] = jnp.zeros_like(impulse)
    geo[...] = jnp.ones_like(geo)

    def keep(flag, value):
        return jnp.where(flag > 0, value, 0.0)

    def put_ghosts(landed, rows):
        lane = lane16 if rows == 16 else lane8
        table[0:rows, 512:640] = jnp.where(
            lane < 64, keep(has_lower_sub, landed[0]), keep(has_higher_sub, landed[1])
        )
        table[0:rows, 640:768] = jnp.where(
            lane < 64, keep(has_lower_layer, landed[2]), keep(has_higher_layer, landed[3])
        )

    for copy in first_trade:
        copy.wait_recv()
    put_ghosts([first_in[slot] for slot in range(4)], 16)

    def pick(component, e):
        high = lax.shift_right_logical(index[e], 7)
        low = lax.bitwise_and(index[e], 127)
        got = None
        for h in range(TABLE if e else OWN):
            row = table[component : component + 1, h * LANES : (h + 1) * LANES]
            block = take(jnp.broadcast_to(row, (ROWS, LANES)), low)
            got = block if h == 0 else jnp.where(high == h, block, got)
        return got

    props_a = [pick(8 + i, 0) for i in range(4)]
    props_b = [pick(8 + i, 1) for i in range(4)]
    for i in range(4):
        const[20 + i] = props_a[i]
        const[24 + i] = props_b[i]

    for step in range(1, WIN):
        relay_copy(step).wait_recv()
    for c in range(10):
        rows = slice(c * TILES, (c + 1) * TILES)
        geo[c, 0:TILES] = (
            outgoing[place, rows] + incoming[0, rows] + incoming[1, rows] + incoming[2, rows]
        )

    raw = [geo[i] for i in range(3)]
    length = jnp.sqrt(dot3(raw, raw))
    normal = [r / length for r in raw]
    side = jnp.sqrt(normal[1] * normal[1] + normal[2] * normal[2])
    one_y = normal[2] / side
    one_z = -normal[1] / side
    two = cross(normal, [jnp.zeros_like(side), one_y, one_z])
    frame = [normal, [jnp.zeros_like(side), one_y, one_z], two]
    entry_a = arm_block([geo[3 + i] for i in range(3)], props_a[1:])
    entry_b = arm_block([geo[6 + i] for i in range(3)], props_b[1:])
    mass = props_a[0] + props_b[0]
    xx, yy, zz, xy, xz, yz = [a + b for a, b in zip(entry_a, entry_b)]
    xx, yy, zz = mass + xx, mass + yy, mass + zz
    cxx = yy * zz - yz * yz
    cxy = xz * yz - xy * zz
    cxz = xy * yz - xz * yy
    cyy = xx * zz - xz * xz
    cyz = xy * xz - xx * yz
    czz = xx * yy - xy * xy
    scale = relaxation / (xx * cxx + xy * cxy + xz * cxz)
    solve = [[cxx, cxy, cxz], [cxy, cyy, cyz], [cxz, cyz, czz]]
    for i in range(3):
        row = [dot3(frame[i], solve[j]) * scale for j in range(3)]
        for j in range(3):
            const[8 + 3 * i + j] = row[j]
        const[17 + i] = dot3(row, normal) * geo[9]
    for i in range(3):
        const[i] = normal[i]
        const[5 + i] = two[i]
    const[3] = one_y
    const[4] = one_z

    def color_pass(color, carry):
        vel_a = [pick(c, 0) for c in range(6)]
        vel_b = [pick(c, 1) for c in range(6)]
        arm_a = [geo[3 + i] for i in range(3)]
        arm_b = [geo[6 + i] for i in range(3)]
        turn_a = cross(vel_a[3:], arm_a)
        turn_b = cross(vel_b[3:], arm_b)
        relative = [vel_a[i] + turn_a[i] - vel_b[i] - turn_b[i] for i in range(3)]
        old = [impulse[i] for i in range(3)]
        trial = [
            old[i]
            - dot3([const[8 + 3 * i + j] for j in range(3)], relative)
            - const[17 + i]
            for i in range(3)
        ]
        press = jnp.maximum(trial[0], 0.0)
        slide = jnp.sqrt(trial[1] * trial[1] + trial[2] * trial[2])
        factor = jnp.minimum(1.0, friction * press / jnp.maximum(slide, tangent_floor))
        active = shade[...] == color
        new = [
            jnp.where(active, value, was)
            for value, was in zip([press, trial[1] * factor, trial[2] * factor], old)
        ]
        change = [a - b for a, b in zip(new, old)]
        for i in range(3):
            impulse[i] = new[i]
        force = [
            const[0] * change[0] + const[5] * change[2],
            const[1] * change[0] + const[3] * change[1] + const[6] * change[2],
            const[2] * change[0] + const[4] * change[1] + const[7] * change[2],
        ]
        torque_a = cross(arm_a, force)
        torque_b = cross(arm_b, force)
        for i in range(3):
            lin = slice(i * TILES, (i + 1) * TILES)
            ang = slice((3 + i) * TILES, (4 + i) * TILES)
            push[0, lin] = (const[20] * force[i])[0:TILES]
            push[1, lin] = (-const[24] * force[i])[0:TILES]
            push[0, ang] = (const[21 + i] * torque_a[i])[0:TILES]
            push[1, ang] = (-const[25 + i] * torque_b[i])[0:TILES]
        for e in range(2):
            for t in range(TILES):
                value = push[e, pl.ds(t, 8, stride=TILES), :]
                upper = coarse(value)
                lower = value - upper
                part = lax.shift_right_logical(index[e, t : t + 1], 8)
                pieces = [
                    jnp.where(part == h, half, 0.0) for half in (upper, lower) for h in range(3)
                ]
                at = (e * TILES + t) * LANES
                push_left[:, at : at + LANES] = jnp.concatenate(pieces, axis=0).astype(BF16)
        total = lax.dot_general(
            push_left[...], pair_hot[...], NT, preferred_element_type=F32
        )
        for h in range(3):
            cols = slice(h * SPLIT, (h + 1) * SPLIT)
            table[0:8, cols] = (
                table[0:8, cols]
                + total[h * 8 : (h + 1) * 8]
                + total[24 + h * 8 : 32 + h * 8]
            )
        return carry

    waiting = list(first_trade)
    for sweep in range(SWEEPS):
        start[...] = table[0:8, :]
        lax.fori_loop(0, NCOLOR, color_pass, 0)
        step = 1 + 2 * sweep
        for pair in range(2):
            cols = slice((OWN + pair) * LANES, (OWN + pair + 1) * LANES)
            round_out[step - 1, pair] = table[0:8, cols] - start[:, cols]
        copies = exchange(step)
        for copy in copies:
            copy.start()
        for copy in copies:
            copy.wait_recv()
        waiting += copies
        arrived = [
            jnp.where(lane8 < 64, round_in[step - 1, 1], round_in[step - 1, 0]),
            jnp.where(lane8 < 64, round_in[step - 1, 3], round_in[step - 1, 2]),
        ]
        for h in range(OWN):
            cols = slice(h * LANES, (h + 1) * LANES)
            total = table[0:8, cols] - start[:, cols]
            for half in range(4):
                spot = inverse_list[h * 4 + half]
                total = total + jnp.where(
                    spot >= 0, take(arrived[half // 2], jnp.maximum(spot, 0)), 0.0
                )
            own = start[:, cols] + total * weight[:, cols]
            table[0:8, cols] = own
            if sweep + 1 == SWEEPS:
                vel_out[pl.ds(h, 6, stride=OWN), :] = own[0:6]
        if sweep + 1 < SWEEPS:
            for pair in range(2):
                round_out[step, pair] = pick_listed(pair, 8)
            copies = exchange(step + 1)
            for copy in copies:
                copy.start()
            for copy in copies:
                copy.wait_recv()
            waiting += copies
            put_ghosts([round_in[step, slot] for slot in range(4)], 8)

    for i in range(3):
        imp_out[i * TILES : (i + 1) * TILES, :] = impulse[i, 0:TILES]
    for copy in waiting:
        copy.wait_send()
    for step in range(1, WIN):
        relay_copy(step).wait_send()


def on_device(n_sub, n_layer, geometry, dest_slot, pairs, colors, free_vel, inertia, exports):
    vmem = pl.BlockSpec(memory_space=pltpu.VMEM)
    impulse, velocity = pl.pallas_call(
        lambda *refs: kernel(n_sub, n_layer, *refs),
        out_shape=(
            jax.ShapeDtypeStruct((3 * TILES, LANES), F32),
            jax.ShapeDtypeStruct((6 * OWN, LANES), F32),
        ),
        in_specs=[vmem, vmem, vmem, pl.BlockSpec(memory_space=pltpu.SMEM), vmem, vmem, vmem],
        out_specs=(vmem, vmem),
        scratch_shapes=[
            pltpu.VMEM((SPLIT, TILES * LANES), BF16),
            pltpu.VMEM((SPLIT, 2 * TILES * LANES), BF16),
            pltpu.VMEM((32, TILES * LANES), F32),
            pltpu.VMEM((192, TILES * LANES), BF16),
            pltpu.VMEM((48, 2 * TILES * LANES), BF16),
            pltpu.VMEM((WIN, 10 * TILES, LANES), F32),
            pltpu.VMEM((WIN - 1, 10 * TILES, LANES), F32),
            pltpu.VMEM((10, ROWS, LANES), F32),
            pltpu.VMEM((2, ROWS, LANES), jnp.int32),
            pltpu.VMEM((ROWS, LANES), jnp.int32),
            pltpu.VMEM((28, ROWS, LANES), F32),
            pltpu.VMEM((3, ROWS, LANES), F32),
            pltpu.VMEM((2, 8 * TILES, LANES), F32),
            pltpu.VMEM((16, TABLE * LANES), F32),
            pltpu.VMEM((8, TABLE * LANES), F32),
            pltpu.VMEM((16, 8, LANES), jnp.int32),
            pltpu.VMEM((8, OWN * LANES), F32),
            pltpu.VMEM((2, 16, LANES), F32),
            pltpu.VMEM((4, 16, LANES), F32),
            pltpu.VMEM((5, 2, 8, LANES), F32),
            pltpu.VMEM((5, 4, 8, LANES), F32),
            pltpu.SemaphoreType.DMA((WIN - 1,)),
            pltpu.SemaphoreType.DMA((WIN - 1,)),
            pltpu.SemaphoreType.DMA((6, 4)),
            pltpu.SemaphoreType.DMA((6, 4)),
        ],
        compiler_params=pltpu.CompilerParams(
            collective_id=0, has_side_effects=True, vmem_limit_bytes=24 << 20
        ),
    )(
        geometry.reshape(10 * TILES, LANES),
        dest_slot.reshape(TILES, LANES),
        pairs.reshape(2 * TILES, LANES),
        colors,
        free_vel.reshape(6 * OWN, LANES),
        inertia.reshape(4 * OWN, LANES),
        exports,
    )
    return impulse.reshape(3, 1, TILES * LANES), velocity.reshape(6, 1, OWN * LANES)


def solution(mesh):
    n_sub, n_layer = mesh.shape["sub"], mesh.shape["layer"]
    placed = (
        P(None, "layer", "sub"),
        P("layer", "sub"),
        P(None, "layer", "sub"),
        P("layer", "sub"),
        P(None, "layer", "sub"),
        P(None, "layer", "sub"),
        P(None, "layer", "sub"),
    )
    return jax.shard_map(
        lambda *arrays: on_device(n_sub, n_layer, *arrays),
        mesh=mesh,
        in_specs=placed,
        out_specs=(P(None, "layer", "sub"), P(None, "layer", "sub")),
        check_vma=False,
    )
```

profile of v0, /device:TPU:8, one launch (start us, length us, event | category | flops | bytes accessed | tf_op | source)
XLA Modules:
  0.0 46.4 jit_solution(11392286691911095487)
XLA Ops:
  0.6 0.0 copy-start.1
  0.6 0.0 copy-start.3
  0.7 0.0 copy-start.4
  0.7 0.7 %reduce = s32[1536]{0:T(1024)S(1)} reduce(s32[1,1536]{1,0:T(1,128)} %param.8, s32[]{:T(128)} %constant.7), dimensions={0}, to_apply=%param.8.reduce_sub_computation | reduce | bytes 12292 | tf_op args[1]
  1.4 0.0 copy-start.5
  1.4 0.0 copy-done.1
  1.4 0.0 copy-done.3
  1.4 0.0 copy-done.4
  1.4 0.6 %copy-done.5 = s32[1,12]{1,0:T(1,128)S(1)} copy-done((s32[1,12]{1,0:T(1,128)S(1)}, s32[1,12]{1,0:T(1,128)}, u32[]{:S(2)}) %copy-start.5) | copy-done | bytes 72
  2.1 0.0 copy-start
  2.1 0.8 %copy-done = f32[10,1,1536]{2,1,0:T(1,128)S(1)} copy-done((f32[10,1,1536]{2,1,0:T(1,128)S(1)}, f32[10,1,1536]{2,1,0:T(1,128)}, u32[]{:S(2)}) %copy-start) | copy-done | bytes 61464
  2.9 0.0 copy-start.2
  2.9 0.7 %copy-done.2 = f32[6,1,512]{2,1,0:T(1,128)S(1)} copy-done((f32[6,1,512]{2,1,0:T(1,128)S(1)}, f32[6,1,512]{2,1,0:T(1,128)}, u32[]{:S(2)}) %copy-start.2) | copy-done | bytes 12312
  3.6 41.5 %shard_map.86 = (f32[36,128]{1,0:T(8,128)S(1)}, f32[24,128]{1,0:T(8,128)S(1)}) custom-call(f32[120,128]{1,0:T(8,128)S(1)} %bitcast.6, s32[12,128]{1,0:T(8,128)S(1)} %bitcast.7, s32[24,128]{1,0:T(8,128)S(1)} %bitcast.8, s32[1,12]{1,0:T(1,128)S(1)} %copy-done.5, f32[24,128]{1,0:T(8,128)S(1)} %bitcast.9, f32[16,128]{1,0:T(8,128)S(1)} %bitcast.11, ...), custom_call_target="tpu_custom_call" | custom-call | tf_op jit(solution)/shard_map/pallas_call | solution.py:464
  45.1 0.6 %reshape.32 = f32[3,1,1536]{2,1,0:T(1,128)} reshape(f32[36,128]{1,0:T(8,128)S(1)} %get-tuple-element.4) | data formatting | bytes 36864 | tf_op jit(solution)/shard_map/reshape | solution.py:511
  45.8 0.6 %copy.14 = f32[6,1,512]{2,1,0:T(1,128)} copy(f32[6,1,512]{2,1,0:T(1,128)S(1)} %bitcast.10) | data formatting | bytes 24576
Async XLA Ops:
  0.6 0.8 %copy-start.1 = (s32[2,1,1536]{2,1,0:T(1,128)S(1)}, s32[2,1,1536]{2,1,0:T(1,128)}, u32[]{:S(2)}) copy-start(s32[2,1,1536]{2,1,0:T(1,128)} %param.9) | copy-start | bytes 36868
  0.6 0.8 %copy-start.3 = (f32[4,1,512]{2,1,0:T(1,128)S(1)}, f32[4,1,512]{2,1,0:T(1,128)}, u32[]{:S(2)}) copy-start(f32[4,1,512]{2,1,0:T(1,128)} %param.12) | copy-start | bytes 24580
  0.7 0.8 %copy-start.4 = (s32[4,1,64]{2,1,0:T(1,128)S(1)}, s32[4,1,64]{2,1,0:T(1,128)}, u32[]{:S(2)}) copy-start(s32[4,1,64]{2,1,0:T(1,128)} %refs_6_.1) | copy-start | bytes 3076
  1.4 0.7 %copy-start.5 = (s32[1,12]{1,0:T(1,128)S(1)}, s32[1,12]{1,0:T(1,128)}, u32[]{:S(2)}) copy-start(s32[1,12]{1,0:T(1,128)} %refs_3_.1) | copy-start | bytes 148
  2.1 0.8 %copy-start = (f32[10,1,1536]{2,1,0:T(1,128)S(1)}, f32[10,1,1536]{2,1,0:T(1,128)}, u32[]{:S(2)}) copy-start(f32[10,1,1536]{2,1,0:T(1,128)} %param.7) | copy-start | bytes 184324
  2.9 0.7 %copy-start.2 = (f32[6,1,512]{2,1,0:T(1,128)S(1)}, f32[6,1,512]{2,1,0:T(1,128)}, u32[]{:S(2)}) copy-start(f32[6,1,512]{2,1,0:T(1,128)} %param.11) | copy-start | bytes 36868
where the time goes:
time: 46.6 us; the launch traced here: 46.4 us
  Pallas kernels  41.5 us (89%)
  local copies, waits for them, and re-layouts  3.39 us (7%)
  other arithmetic  0.73 us (2%)
  between operations  0.7 us (2%)
    pallas_call x1, Pallas kernels, on_device(): pl.pallas_call(lambda *refs: kernel(n_sub, n_layer, *refs), out_shape=(ja...  41.5 us
    unnamed x13, local copies, waits for them, and re-layouts  2.77 us

commit v1 on v0

--- a/solution.py
+++ b/solution.py
@@ -59,6 +59,15 @@
 def kernel(
     n_sub,
     n_layer,
+    geo_hbm,
+    slot_hbm,
+    pairs_hbm,
+    color_hbm,
+    free_hbm,
+    inertia_hbm,
+    exports_hbm,
+    imp_out,
+    vel_out,
     geo_ref,
     slot_ref,
     pairs_ref,
@@ -66,8 +75,7 @@
     free_ref,
     inertia_ref,
     exports_ref,
-    imp_out,
-    vel_out,
+    load_sem,
     slot_hot,
     pair_hot,
     split_geo,
@@ -121,6 +129,23 @@
             barrier, inc=1, device_id=(mate(step), layer), device_id_type=MESH
         )
 
+    loads = [
+        pltpu.make_async_copy(src, dst, load_sem.at[i])
+        for i, (src, dst) in enumerate(
+            (
+                (free_hbm, free_ref),
+                (inertia_hbm, inertia_ref),
+                (exports_hbm, exports_ref),
+                (geo_hbm, geo_ref),
+                (slot_hbm.at[:, 0, :], slot_ref),
+                (pairs_hbm, pairs_ref),
+                (color_hbm, color_ref),
+            )
+        )
+    ]
+    for load in loads:
+        load.start()
+
     def trade(step, src, dst):
         return [
             pltpu.make_async_remote_copy(
@@ -141,6 +166,8 @@
     lane16 = lax.broadcasted_iota(jnp.int32, (ROWS, LANES), 1)
 
     table[...] = jnp.zeros_like(table)
+    for load in loads[0:3]:
+        load.wait()
     for h in range(OWN):
         cols = slice(h * LANES, (h + 1) * LANES)
         table[0:6, cols] = free_ref[pl.ds(h, 6, stride=OWN), :]
@@ -162,6 +189,8 @@
     for pair in range(2):
         first_out[pair] = pick_listed(pair, 16)
 
+    for load in loads[3:]:
+        load.wait()
     for t in range(TILES):
         cols = slice(t * LANES, (t + 1) * LANES)
         main = geo_ref[pl.ds(t, 8, stride=TILES), :]
@@ -232,12 +261,12 @@
     index[...] = jnp.zeros_like(index)
     for e in range(2):
         index[e, 0:TILES] = pairs_ref[e * TILES : (e + 1) * TILES, :]
-        for t in range(TILES):
-            low = lax.bitwise_and(
-                pairs_ref[e * TILES + t : e * TILES + t + 1, :], SPLIT - 1
-            )
-            at = (e * TILES + t) * LANES
-            pair_hot[:, at : at + LANES] = (spread == low).astype(F32).astype(BF16)
+    upright = jnp.transpose(lax.bitwise_and(pairs_ref[...], SPLIT - 1).astype(F32))
+    along = lax.broadcasted_iota(jnp.int32, (LANES, SPLIT), 1).astype(F32)
+    for t in range(2 * TILES):
+        pair_hot[t * LANES : (t + 1) * LANES, :] = (
+            (along == upright[:, t : t + 1]).astype(F32).astype(BF16)
+        )
     row16 = lax.broadcasted_iota(jnp.int32, (ROWS, LANES), 0)
     tint = jnp.full((ROWS, LANES), -1, jnp.int32)
     for t in range(TILES):
@@ -398,9 +427,7 @@
                 ]
                 at = (e * TILES + t) * LANES
                 push_left[:, at : at + LANES] = jnp.concatenate(pieces, axis=0).astype(BF16)
-        total = lax.dot_general(
-            push_left[...], pair_hot[...], NT, preferred_element_type=F32
-        )
+        total = jnp.dot(push_left[...], pair_hot[...], preferred_element_type=F32)
         for h in range(3):
             cols = slice(h * SPLIT, (h + 1) * SPLIT)
             table[0:8, cols] = (
@@ -410,8 +437,7 @@
             )
         return carry
 
-    waiting = list(first_trade)
-    for sweep in range(SWEEPS):
+    def one_sweep(sweep, carry):
         start[...] = table[0:8, :]
         lax.fori_loop(0, NCOLOR, color_pass, 0)
         step = 1 + 2 * sweep
@@ -423,7 +449,6 @@
             copy.start()
         for copy in copies:
             copy.wait_recv()
-        waiting += copies
         arrived = [
             jnp.where(lane8 < 64, round_in[step - 1, 1], round_in[step - 1, 0]),
             jnp.where(lane8 < 64, round_in[step - 1, 3], round_in[step - 1, 2]),
@@ -436,24 +461,31 @@
                 total = total + jnp.where(
                     spot >= 0, take(arrived[half // 2], jnp.maximum(spot, 0)), 0.0
                 )
-            own = start[:, cols] + total * weight[:, cols]
-            table[0:8, cols] = own
-            if sweep + 1 == SWEEPS:
-                vel_out[pl.ds(h, 6, stride=OWN), :] = own[0:6]
-        if sweep + 1 < SWEEPS:
+            table[0:8, cols] = start[:, cols] + total * weight[:, cols]
+        for copy in copies:
+            copy.wait_send()
+
+        @pl.when(sweep + 1 < SWEEPS)
+        def _():
             for pair in range(2):
                 round_out[step, pair] = pick_listed(pair, 8)
-            copies = exchange(step + 1)
-            for copy in copies:
+            back = exchange(step + 1)
+            for copy in back:
                 copy.start()
-            for copy in copies:
+            for copy in back:
                 copy.wait_recv()
-            waiting += copies
             put_ghosts([round_in[step, slot] for slot in range(4)], 8)
-
+            for copy in back:
+                copy.wait_send()
+
+        return carry
+
+    lax.fori_loop(0, SWEEPS, one_sweep, 0)
+    for h in range(OWN):
+        vel_out[pl.ds(h, 6, stride=OWN), :] = table[0:6, h * LANES : (h + 1) * LANES]
     for i in range(3):
         imp_out[i * TILES : (i + 1) * TILES, :] = impulse[i, 0:TILES]
-    for copy in waiting:
+    for copy in first_trade:
         copy.wait_send()
     for step in range(1, WIN):
         relay_copy(step).wait_send()
@@ -461,17 +493,26 @@
 
 def on_device(n_sub, n_layer, geometry, dest_slot, pairs, colors, free_vel, inertia, exports):
     vmem = pl.BlockSpec(memory_space=pltpu.VMEM)
+    hbm = pl.BlockSpec(memory_space=pltpu.HBM)
     impulse, velocity = pl.pallas_call(
         lambda *refs: kernel(n_sub, n_layer, *refs),
         out_shape=(
             jax.ShapeDtypeStruct((3 * TILES, LANES), F32),
             jax.ShapeDtypeStruct((6 * OWN, LANES), F32),
         ),
-        in_specs=[vmem, vmem, vmem, pl.BlockSpec(memory_space=pltpu.SMEM), vmem, vmem, vmem],
+        in_specs=[hbm] * 7,
         out_specs=(vmem, vmem),
         scratch_shapes=[
+            pltpu.VMEM((10 * TILES, LANES), F32),
+            pltpu.VMEM((TILES, LANES), jnp.int32),
+            pltpu.VMEM((2 * TILES, LANES), jnp.int32),
+            pltpu.SMEM((1, TILES), jnp.int32),
+            pltpu.VMEM((6 * OWN, LANES), F32),
+            pltpu.VMEM((4 * OWN, LANES), F32),
+            pltpu.VMEM((4, 1, 64), jnp.int32),
+            pltpu.SemaphoreType.DMA((7,)),
             pltpu.VMEM((SPLIT, TILES * LANES), BF16),
-            pltpu.VMEM((SPLIT, 2 * TILES * LANES), BF16),
+            pltpu.VMEM((2 * TILES * LANES, SPLIT), BF16),
             pltpu.VMEM((32, TILES * LANES), F32),
             pltpu.VMEM((192, TILES * LANES), BF16),
             pltpu.VMEM((48, 2 * TILES * LANES), BF16),
@@ -497,11 +538,11 @@
             pltpu.SemaphoreType.DMA((6, 4)),
         ],
         compiler_params=pltpu.CompilerParams(
-            collective_id=0, has_side_effects=True, vmem_limit_bytes=24 << 20
+            collective_id=0, has_side_effects=True, vmem_limit_bytes=60 << 20
         ),
     )(
         geometry.reshape(10 * TILES, LANES),
-        dest_slot.reshape(TILES, LANES),
+        dest_slot.reshape(TILES, 1, LANES),
         pairs.reshape(2 * TILES, LANES),
         colors,
         free_vel.reshape(6 * OWN, LANES),

time: 46.6 us -> 42.6 us (0.914)
  Pallas kernels: 41.5 us -> 39.8 us
  local copies, waits for them, and re-layouts: 3.39 us -> 1.96 us
  other arithmetic: 0.73 us -> 0 us
    unnamed x13 -> x3, local copies, waits for them, and re-layouts: 2.77 us -> 0.6 us
    pallas_call x1, Pallas kernels: 41.5 us -> 39.8 us  [on_device(): pl.pallas_call(lambda *refs: kernel(n_sub, n_layer, *refs), out_shape=(ja...]
    reshape x1, local copies, waits for them, and re-layouts: 0.63 us -> 1.36 us  [on_device(): impulse.reshape(3, 1, TILES * LANES)]
    unnamed x1 -> x0, other arithmetic: 0.73 us -> none
where the time goes in v1:
time: 42.6 us; the launch traced here: 42.4 us
  Pallas kernels  39.8 us (93%)
  local copies, waits for them, and re-layouts  1.96 us (5%)
  between operations  0.65 us (2%)
    pallas_call x1, Pallas kernels, on_device(): pl.pallas_call(lambda *refs: kernel(n_sub, n_layer, *refs), out_shape=(ja...  39.8 us
    reshape x1, local copies, waits for them, and re-layouts, on_device(): impulse.reshape(3, 1, TILES * LANES)  1.36 us

profile of v1, /device:TPU:8, one launch (start us, length us, event | category | flops | bytes accessed | tf_op | source)
XLA Modules:
  0.0 42.4 jit_solution(8545510135877335481)
XLA Ops:
  0.6 39.8 %shard_map.86 = (f32[36,128]{1,0:T(8,128)}, f32[24,128]{1,0:T(8,128)}) custom-call(f32[120,128]{1,0:T(8,128)} %bitcast.6, s32[12,1,128]{2,1,0:T(1,128)} %bitcast.11, s32[24,128]{1,0:T(8,128)} %bitcast.7, s32[1,12]{1,0:T(1,128)} %refs_3_.1, f32[24,128]{1,0:T(8,128)} %bitcast.8, f32[16,128]{1,0:T(8,128)} %bitcast.10, s32[4,1,64]{2,1,0:T(1,128)} %refs_6_.1), custom_call_target="tpu_custom_call" | custom-call | tf_op jit(solution)/shard_map/pallas_call | solution.py:497
  40.4 0.0 copy-start
  40.4 1.4 %reshape.32 = f32[3,1,1536]{2,1,0:T(1,128)} reshape(f32[36,128]{1,0:T(8,128)} %get-tuple-element.4) | data formatting | bytes 36864 | tf_op jit(solution)/shard_map/reshape | solution.py:552
  41.8 0.0 copy-done
  41.8 0.6 %copy.14 = f32[6,1,512]{2,1,0:T(1,128)} copy(f32[6,1,512]{2,1,0:T(1,128)S(1)} %bitcast.9) | data formatting | bytes 24576
Async XLA Ops:
  40.4 1.4 %copy-start = (f32[24,128]{1,0:T(8,128)S(1)}, f32[24,128]{1,0:T(8,128)}, u32[]{:S(2)}) copy-start(f32[24,128]{1,0:T(8,128)} %get-tuple-element.5) | copy-start | bytes 36868

commit v2 on v1

--- a/solution.py
+++ b/solution.py
@@ -19,6 +19,7 @@
 friction = 0.6
 tangent_floor = 0.1
 
+FAR = ((-2, 0), (2, 0), (0, -2), (0, 2), (-1, -1), (-1, 1), (1, -1), (1, 1))
 MESH = pl.DeviceIdType.MESH
 F32 = jnp.float32
 BF16 = jnp.bfloat16
@@ -95,12 +96,19 @@
     weight,
     first_out,
     first_in,
-    round_out,
-    round_in,
+    info,
+    info_out,
+    info_in,
+    hints,
+    sweep_out,
+    near_in,
+    far_in,
     relay_send,
     relay_recv,
-    round_send,
-    round_recv,
+    near_send,
+    near_recv,
+    far_send,
+    far_recv,
 ):
     sub = lax.axis_index("sub")
     layer = lax.axis_index("layer")
@@ -121,8 +129,18 @@
         ((sub, higher_layer), 2, 1),
     )
 
+    far = tuple(
+        (
+            (lax.rem(sub + n_sub + right, n_sub), lax.rem(layer + n_layer + up, n_layer)),
+            FAR.index((-right, -up)),
+            2 if right == 0 else 1,
+            1 if right == 0 or up == 0 else 2,
+        )
+        for right, up in FAR
+    )
+
     barrier = pltpu.get_barrier_semaphore()
-    for device, _, _ in around:
+    for device in [a[0] for a in around] + [f[0] for f in far]:
         pl.semaphore_signal(barrier, inc=1, device_id=device, device_id_type=MESH)
     for step in range(1, WIN):
         pl.semaphore_signal(
@@ -146,21 +164,36 @@
     for load in loads:
         load.start()
 
-    def trade(step, src, dst):
+    def trade(step, source_of, dst):
         return [
             pltpu.make_async_remote_copy(
-                src_ref=src.at[pair],
+                src_ref=source_of(pair),
                 dst_ref=dst.at[slot],
-                send_sem=round_send.at[step, slot],
-                recv_sem=round_recv.at[step, slot],
+                send_sem=near_send.at[step, slot],
+                recv_sem=near_recv.at[step, slot],
                 device_id=device,
                 device_id_type=MESH,
             )
             for device, slot, pair in around
         ]
 
-    def exchange(step):
-        return trade(step, round_out.at[step - 1], round_in.at[step - 1])
+    def near_copies(sweep):
+        return trade(
+            2 + sweep, lambda pair: sweep_out.at[sweep, pl.ds(2 * pair, 2)], near_in.at[sweep]
+        )
+
+    def far_copies(sweep):
+        return [
+            pltpu.make_async_remote_copy(
+                src_ref=sweep_out.at[sweep, pl.ds(first, count)],
+                dst_ref=far_in.at[sweep, slot, pl.ds(0, count)],
+                send_sem=far_send.at[sweep, slot],
+                recv_sem=far_recv.at[sweep, slot],
+                device_id=device,
+                device_id_type=MESH,
+            )
+            for device, slot, first, count in far
+        ]
 
     lane8 = lax.broadcasted_iota(jnp.int32, (8, LANES), 1)
     lane16 = lax.broadcasted_iota(jnp.int32, (ROWS, LANES), 1)
@@ -177,12 +210,12 @@
         jnp.concatenate([exports_ref[3], exports_ref[2]], axis=1),
     ]
 
-    def pick_listed(pair, rows):
+    def pick_listed(pair, rows, source=table):
         high = jnp.broadcast_to(lax.shift_right_logical(listed[pair], 7), (rows, LANES))
         low = jnp.broadcast_to(lax.bitwise_and(listed[pair], 127), (rows, LANES))
-        got = take(table[0:rows, 0:LANES], low)
+        got = take(source[0:rows, 0:LANES], low)
         for h in range(1, OWN):
-            block = take(table[0:rows, h * LANES : (h + 1) * LANES], low)
+            block = take(source[0:rows, h * LANES : (h + 1) * LANES], low)
             got = jnp.where(high == h, block, got)
         return got
 
@@ -212,8 +245,8 @@
         low = lax.bitwise_and(slot_ref[t : t + 1, :], SPLIT - 1)
         slot_hot[:, t * LANES : (t + 1) * LANES] = (spread == low).astype(F32).astype(BF16)
 
-    pl.semaphore_wait(barrier, 7)
-    first_trade = trade(0, first_out, first_in)
+    pl.semaphore_wait(barrier, 15)
+    first_trade = trade(0, lambda pair: first_out.at[pair], first_in)
     for copy in first_trade:
         copy.start()
 
@@ -298,8 +331,15 @@
             spot = jnp.broadcast_to(found[half : half + 1, cols], (8, LANES))
             spot = spot.astype(jnp.int32) * exists[half] - 1
             inverse_list[h * 4 + half] = spot
+            info[half : half + 1, cols] = spot[0:1].astype(F32)
             times = times + jnp.where(spot >= 0, 1.0, 0.0)
         weight[:, cols] = 1.0 / times
+        info[4:8, cols] = (1.0 / times)[0:4]
+    for pair in range(2):
+        info_out[pair] = pick_listed(pair, 8, info)
+    info_trade = trade(1, lambda pair: info_out.at[pair], info_in)
+    for copy in info_trade:
+        copy.start()
     push[...] = jnp.zeros_like(push)
     impulse[...] = jnp.zeros_like(impulse)
     geo[...] = jnp.ones_like(geo)
@@ -307,18 +347,19 @@
     def keep(flag, value):
         return jnp.where(flag > 0, value, 0.0)
 
-    def put_ghosts(landed, rows):
-        lane = lane16 if rows == 16 else lane8
-        table[0:rows, 512:640] = jnp.where(
-            lane < 64, keep(has_lower_sub, landed[0]), keep(has_higher_sub, landed[1])
-        )
-        table[0:rows, 640:768] = jnp.where(
-            lane < 64, keep(has_lower_layer, landed[2]), keep(has_higher_layer, landed[3])
+    def halves(lane, landed):
+        return (
+            jnp.where(
+                lane < 64, keep(has_lower_sub, landed[0]), keep(has_higher_sub, landed[1])
+            ),
+            jnp.where(
+                lane < 64, keep(has_lower_layer, landed[2]), keep(has_higher_layer, landed[3])
+            ),
         )
 
     for copy in first_trade:
         copy.wait_recv()
-    put_ghosts([first_in[slot] for slot in range(4)], 16)
+    table[:, 512:640], table[:, 640:768] = halves(lane16, [first_in[slot] for slot in range(4)])
 
     def pick(component, e):
         high = lax.shift_right_logical(index[e], 7)
@@ -437,21 +478,37 @@
             )
         return carry
 
+    for copy in info_trade:
+        copy.wait_recv()
+    hints[0], hints[1] = halves(lane8, [info_in[slot] for slot in range(4)])
+
+    def pull(row_block, pair, row):
+        spot = jnp.broadcast_to(hints[pair, row : row + 1], (8, LANES)).astype(jnp.int32)
+        return jnp.where(spot >= 0, take(row_block, jnp.maximum(spot, 0)), 0.0)
+
     def one_sweep(sweep, carry):
         start[...] = table[0:8, :]
         lax.fori_loop(0, NCOLOR, color_pass, 0)
-        step = 1 + 2 * sweep
+        on = sweep + 1 < SWEEPS
+        copied = [slice((OWN + pair) * LANES, (OWN + pair + 1) * LANES) for pair in range(2)]
         for pair in range(2):
-            cols = slice((OWN + pair) * LANES, (OWN + pair + 1) * LANES)
-            round_out[step - 1, pair] = table[0:8, cols] - start[:, cols]
-        copies = exchange(step)
-        for copy in copies:
+            sweep_out[sweep, 1 + pair] = table[0:8, copied[pair]] - start[:, copied[pair]]
+
+        @pl.when(on)
+        def _():
+            for copy in far_copies(sweep):
+                copy.start()
+
+        for pair in range(2):
+            sweep_out[sweep, 3 * pair] = pick_listed(pair, 8)
+        near = near_copies(sweep)
+        for copy in near:
             copy.start()
-        for copy in copies:
+        for copy in near:
             copy.wait_recv()
         arrived = [
-            jnp.where(lane8 < 64, round_in[step - 1, 1], round_in[step - 1, 0]),
-            jnp.where(lane8 < 64, round_in[step - 1, 3], round_in[step - 1, 2]),
+            jnp.where(lane8 < 64, near_in[sweep, 1, 1], near_in[sweep, 0, 1]),
+            jnp.where(lane8 < 64, near_in[sweep, 3, 0], near_in[sweep, 2, 0]),
         ]
         for h in range(OWN):
             cols = slice(h * LANES, (h + 1) * LANES)
@@ -462,22 +519,43 @@
                     spot >= 0, take(arrived[half // 2], jnp.maximum(spot, 0)), 0.0
                 )
             table[0:8, cols] = start[:, cols] + total * weight[:, cols]
-        for copy in copies:
+
+        @pl.when(on)
+        def _():
+            for copy in far_copies(sweep):
+                copy.wait_recv()
+
+            def landed(right, up, pair):
+                straight = right == 0 or up == 0
+                return far_in[sweep, FAR.index((right, up)), 0 if straight else pair]
+
+            left = lane8 < 64
+            for pair in range(2):
+                if pair == 0:
+                    listed_now = jnp.where(left, near_in[sweep, 0, 0], near_in[sweep, 1, 0])
+                    beyond = jnp.where(left, landed(2, 0, 0), landed(-2, 0, 0))
+                    side_a = jnp.where(left, landed(-1, 1, 1), landed(-1, -1, 1))
+                    side_b = jnp.where(left, landed(1, 1, 1), landed(1, -1, 1))
+                else:
+                    listed_now = jnp.where(left, near_in[sweep, 2, 1], near_in[sweep, 3, 1])
+                    beyond = jnp.where(left, landed(0, 2, 1), landed(0, -2, 1))
+                    side_a = jnp.where(left, landed(1, -1, 0), landed(-1, -1, 0))
+                    side_b = jnp.where(left, landed(1, 1, 0), landed(-1, 1, 0))
+                was = start[:, copied[pair]]
+                total = (listed_now - was) + sweep_out[sweep, 1 + pair]
+                total = total + jnp.where(
+                    left, pull(beyond, pair, 2 * pair + 1), pull(beyond, pair, 2 * pair)
+                )
+                for row in (2 - 2 * pair, 3 - 2 * pair):
+                    total = total + jnp.where(
+                        left, pull(side_a, pair, row), pull(side_b, pair, row)
+                    )
+                table[0:8, copied[pair]] = was + total * hints[pair, 4:5]
+            for copy in far_copies(sweep):
+                copy.wait_send()
+
+        for copy in near:
             copy.wait_send()
-
-        @pl.when(sweep + 1 < SWEEPS)
-        def _():
-            for pair in range(2):
-                round_out[step, pair] = pick_listed(pair, 8)
-            back = exchange(step + 1)
-            for copy in back:
-                copy.start()
-            for copy in back:
-                copy.wait_recv()
-            put_ghosts([round_in[step, slot] for slot in range(4)], 8)
-            for copy in back:
-                copy.wait_send()
-
         return carry
 
     lax.fori_loop(0, SWEEPS, one_sweep, 0)
@@ -485,7 +563,7 @@
         vel_out[pl.ds(h, 6, stride=OWN), :] = table[0:6, h * LANES : (h + 1) * LANES]
     for i in range(3):
         imp_out[i * TILES : (i + 1) * TILES, :] = impulse[i, 0:TILES]
-    for copy in first_trade:
+    for copy in first_trade + info_trade:
         copy.wait_send()
     for step in range(1, WIN):
         relay_copy(step).wait_send()
@@ -530,12 +608,19 @@
             pltpu.VMEM((8, OWN * LANES), F32),
             pltpu.VMEM((2, 16, LANES), F32),
             pltpu.VMEM((4, 16, LANES), F32),
-            pltpu.VMEM((5, 2, 8, LANES), F32),
-            pltpu.VMEM((5, 4, 8, LANES), F32),
+            pltpu.VMEM((8, OWN * LANES), F32),
+            pltpu.VMEM((2, 8, LANES), F32),
+            pltpu.VMEM((4, 8, LANES), F32),
+            pltpu.VMEM((2, 8, LANES), F32),
+            pltpu.VMEM((SWEEPS, 4, 8, LANES), F32),
+            pltpu.VMEM((SWEEPS, 4, 2, 8, LANES), F32),
+            pltpu.VMEM((SWEEPS - 1, 8, 2, 8, LANES), F32),
             pltpu.SemaphoreType.DMA((WIN - 1,)),
             pltpu.SemaphoreType.DMA((WIN - 1,)),
-            pltpu.SemaphoreType.DMA((6, 4)),
-            pltpu.SemaphoreType.DMA((6, 4)),
+            pltpu.SemaphoreType.DMA((2 + SWEEPS, 4)),
+            pltpu.SemaphoreType.DMA((2 + SWEEPS, 4)),
+            pltpu.SemaphoreType.DMA((SWEEPS - 1, 8)),
+            pltpu.SemaphoreType.DMA((SWEEPS - 1, 8)),
         ],
         compiler_params=pltpu.CompilerParams(
             collective_id=0, has_side_effects=True, vmem_limit_bytes=60 << 20

time: 42.6 us -> 40.1 us (0.941)
  Pallas kernels: 39.8 us -> 37.3 us
    pallas_call x1, Pallas kernels: 39.8 us -> 37.3 us  [on_device(): pl.pallas_call(lambda *refs: kernel(n_sub, n_layer, *refs), out_shape=(ja...]
where the time goes in v2:
time: 40.1 us; the launch traced here: 39.9 us
  Pallas kernels  37.3 us (93%)
  local copies, waits for them, and re-layouts  1.96 us (5%)
  between operations  0.65 us (2%)
    pallas_call x1, Pallas kernels, on_device(): pl.pallas_call(lambda *refs: kernel(n_sub, n_layer, *refs), out_shape=(ja...  37.3 us
    reshape x1, local copies, waits for them, and re-layouts, on_device(): impulse.reshape(3, 1, TILES * LANES)  1.36 us

profile of v2, /device:TPU:8, one launch (start us, length us, event | category | flops | bytes accessed | tf_op | source)
XLA Modules:
  0.0 39.9 jit_solution(14029375448271223328)
XLA Ops:
  0.6 37.3 %shard_map.86 = (f32[36,128]{1,0:T(8,128)}, f32[24,128]{1,0:T(8,128)}) custom-call(f32[120,128]{1,0:T(8,128)} %bitcast.6, s32[12,1,128]{2,1,0:T(1,128)} %bitcast.11, s32[24,128]{1,0:T(8,128)} %bitcast.7, s32[1,12]{1,0:T(1,128)} %refs_3_.1, f32[24,128]{1,0:T(8,128)} %bitcast.8, f32[16,128]{1,0:T(8,128)} %bitcast.10, s32[4,1,64]{2,1,0:T(1,128)} %refs_6_.1), custom_call_target="tpu_custom_call" | custom-call | tf_op jit(solution)/shard_map/pallas_call | solution.py:575
  37.9 0.0 copy-start
  37.9 1.4 %reshape.32 = f32[3,1,1536]{2,1,0:T(1,128)} reshape(f32[36,128]{1,0:T(8,128)} %get-tuple-element.4) | data formatting | bytes 36864 | tf_op jit(solution)/shard_map/reshape | solution.py:637
  39.3 0.0 copy-done
  39.3 0.6 %copy.14 = f32[6,1,512]{2,1,0:T(1,128)} copy(f32[6,1,512]{2,1,0:T(1,128)S(1)} %bitcast.9) | data formatting | bytes 24576
Async XLA Ops:
  37.9 1.4 %copy-start = (f32[24,128]{1,0:T(8,128)S(1)}, f32[24,128]{1,0:T(8,128)}, u32[]{:S(2)}) copy-start(f32[24,128]{1,0:T(8,128)} %get-tuple-element.5) | copy-start | bytes 36868

commit v3 on v2

--- a/solution.py
+++ b/solution.py
@@ -140,7 +140,7 @@
     )
 
     barrier = pltpu.get_barrier_semaphore()
-    for device in [a[0] for a in around] + [f[0] for f in far]:
+    for device, _, _ in around:
         pl.semaphore_signal(barrier, inc=1, device_id=device, device_id_type=MESH)
     for step in range(1, WIN):
         pl.semaphore_signal(
@@ -240,12 +240,18 @@
         split_geo[28:30, cols] = rest - rest_a - rest_b
         split_geo[30:32, cols] = jnp.zeros((2, LANES), F32)
 
-    spread = lax.broadcasted_iota(jnp.int32, (SPLIT, LANES), 0)
-    for t in range(TILES):
-        low = lax.bitwise_and(slot_ref[t : t + 1, :], SPLIT - 1)
-        slot_hot[:, t * LANES : (t + 1) * LANES] = (spread == low).astype(F32).astype(BF16)
-
-    pl.semaphore_wait(barrier, 15)
+    along = lax.broadcasted_iota(jnp.int32, (LANES, SPLIT), 1).astype(F32)
+
+    def upright_hot(codes, hot):
+        upright = jnp.transpose(lax.bitwise_and(codes, SPLIT - 1).astype(F32))
+        for t in range(codes.shape[0]):
+            hot[t * LANES : (t + 1) * LANES, :] = (
+                (along == upright[:, t : t + 1]).astype(F32).astype(BF16)
+            )
+
+    upright_hot(slot_ref[...], slot_hot)
+
+    pl.semaphore_wait(barrier, 7)
     first_trade = trade(0, lambda pair: first_out.at[pair], first_in)
     for copy in first_trade:
         copy.start()
@@ -270,9 +276,7 @@
                 relay_left[g * 32 : (g + 1) * 32, cols] = jnp.where(
                     part == g, values, 0.0
                 ).astype(BF16)
-        placed = lax.dot_general(
-            relay_left[...], slot_hot[...], NT, preferred_element_type=F32
-        )
+        placed = jnp.dot(relay_left[...], slot_hot[...], preferred_element_type=F32)
         for g in range(TABLE):
             block = placed[g * 32 : (g + 1) * 32]
             main = block[0:8] + block[8:16] + block[16:24]
@@ -283,23 +287,20 @@
                 outgoing[target, pl.ds(t, 8, stride=TILES), :] = main[:, cols]
                 outgoing[target, pl.ds(8 * TILES + t, 2, stride=TILES), :] = rest[:, cols]
 
-    def send_part(step, carry):
+    def send_part(turn, carry):
+        swing = 1 - 2 * lax.rem(place, 2)
+        step = 2 + swing * lax.rem(turn, 2) - swing * (turn // 2)
         arrange(lax.rem(place + step, WIN))
         relay_copy(step).start()
         return carry
 
-    lax.fori_loop(1, WIN, send_part, 0)
+    lax.fori_loop(0, WIN - 1, send_part, 0)
     arrange(place)
 
     index[...] = jnp.zeros_like(index)
     for e in range(2):
         index[e, 0:TILES] = pairs_ref[e * TILES : (e + 1) * TILES, :]
-    upright = jnp.transpose(lax.bitwise_and(pairs_ref[...], SPLIT - 1).astype(F32))
-    along = lax.broadcasted_iota(jnp.int32, (LANES, SPLIT), 1).astype(F32)
-    for t in range(2 * TILES):
-        pair_hot[t * LANES : (t + 1) * LANES, :] = (
-            (along == upright[:, t : t + 1]).astype(F32).astype(BF16)
-        )
+    upright_hot(pairs_ref[...], pair_hot)
     row16 = lax.broadcasted_iota(jnp.int32, (ROWS, LANES), 0)
     tint = jnp.full((ROWS, LANES), -1, jnp.int32)
     for t in range(TILES):
@@ -589,7 +590,7 @@
             pltpu.VMEM((4 * OWN, LANES), F32),
             pltpu.VMEM((4, 1, 64), jnp.int32),
             pltpu.SemaphoreType.DMA((7,)),
-            pltpu.VMEM((SPLIT, TILES * LANES), BF16),
+            pltpu.VMEM((TILES * LANES, SPLIT), BF16),
             pltpu.VMEM((2 * TILES * LANES, SPLIT), BF16),
             pltpu.VMEM((32, TILES * LANES), F32),
             pltpu.VMEM((192, TILES * LANES), BF16),
@@ -623,16 +624,21 @@
             pltpu.SemaphoreType.DMA((SWEEPS - 1, 8)),
         ],
         compiler_params=pltpu.CompilerParams(
-            collective_id=0, has_side_effects=True, vmem_limit_bytes=60 << 20
+            collective_id=0, has_side_effects=True, vmem_limit_bytes=32 << 20
         ),
     )(
-        geometry.reshape(10 * TILES, LANES),
-        dest_slot.reshape(TILES, 1, LANES),
-        pairs.reshape(2 * TILES, LANES),
-        colors,
-        free_vel.reshape(6 * OWN, LANES),
-        inertia.reshape(4 * OWN, LANES),
-        exports,
+        *(
+            pltpu.with_memory_space_constraint(array, pltpu.HBM)
+            for array in (
+                geometry.reshape(10 * TILES, LANES),
+                dest_slot.reshape(TILES, 1, LANES),
+                pairs.reshape(2 * TILES, LANES),
+                colors,
+                free_vel.reshape(6 * OWN, LANES),
+                inertia.reshape(4 * OWN, LANES),
+                exports,
+            )
+        )
     )
     return impulse.reshape(3, 1, TILES * LANES), velocity.reshape(6, 1, OWN * LANES)
 

time: 40.1 us -> 37.9 us (0.945)
  Pallas kernels: 37.3 us -> 35.9 us
  local copies, waits for them, and re-layouts: 1.96 us -> 1.22 us
    pallas_call x1, Pallas kernels: 37.3 us -> 35.9 us  [on_device(): pl.pallas_call(lambda *refs: kernel(n_sub, n_layer, *refs), out_shape=(ja...]
    reshape x1, local copies, waits for them, and re-layouts: 1.36 us -> 0.63 us  [on_device(): impulse.reshape(3, 1, TILES * LANES)]
where the time goes in v3:
time: 37.9 us; the launch traced here: 37.8 us
  Pallas kernels  35.9 us (95%)
  local copies, waits for them, and re-layouts  1.22 us (3%)
  between operations  0.64 us (2%)
    pallas_call x1, Pallas kernels, on_device(): pl.pallas_call(lambda *refs: kernel(n_sub, n_layer, *refs), out_shape=(ja...  35.9 us

profile of v3, /device:TPU:8, one launch (start us, length us, event | category | flops | bytes accessed | tf_op | source)
XLA Modules:
  0.0 37.8 jit_solution(12902826008019081430)
XLA Ops:
  0.6 35.9 %shard_map.86 = (f32[36,128]{1,0:T(8,128)S(1)}, f32[24,128]{1,0:T(8,128)S(1)}) custom-call(f32[120,128]{1,0:T(8,128)} %bitcast.7, s32[12,1,128]{2,1,0:T(1,128)} %bitcast.11, s32[24,128]{1,0:T(8,128)} %bitcast.8, s32[1,12]{1,0:T(1,128)} %refs_3_.1, f32[24,128]{1,0:T(8,128)} %bitcast.9, f32[16,128]{1,0:T(8,128)} %bitcast.10, s32[4,1,64]{2,1,0:T(1,128)} %refs_6_.1), custom_call_target="tpu_custom_call" | custom-call | tf_op jit(solution)/shard_map/pallas_call | solution.py:576
  36.6 0.6 %reshape.32 = f32[3,1,1536]{2,1,0:T(1,128)} reshape(f32[36,128]{1,0:T(8,128)S(1)} %get-tuple-element.4) | data formatting | bytes 36864 | tf_op jit(solution)/shard_map/reshape | solution.py:643
  37.2 0.6 %copy.14 = f32[6,1,512]{2,1,0:T(1,128)} copy(f32[6,1,512]{2,1,0:T(1,128)S(1)} %bitcast.6) | data formatting | bytes 24576

commit v4 on v3

--- a/solution.py
+++ b/solution.py
@@ -11,6 +11,7 @@
 LANES = 128
 TILES = 12
 ROWS = 16
+CHUNK = 2
 SPLIT = 256
 OWN = 4
 TABLE = 6
@@ -81,7 +82,7 @@
     pair_hot,
     split_geo,
     relay_left,
-    push_left,
+    block_of,
     outgoing,
     incoming,
     geo,
@@ -270,12 +271,13 @@
         for t in range(TILES):
             cols = slice(t * LANES, (t + 1) * LANES)
             part = lax.shift_right_logical(slot_ref[t : t + 1, :], 8)
-            part = part - (base + target) * TABLE
-            values = split_geo[:, cols]
+            part = (part - (base + target) * TABLE).astype(F32)
+            part = jnp.broadcast_to(part, (32, LANES)).astype(BF16)
+            values = split_geo[:, cols].astype(BF16)
             for g in range(TABLE):
                 relay_left[g * 32 : (g + 1) * 32, cols] = jnp.where(
-                    part == g, values, 0.0
-                ).astype(BF16)
+                    part == jnp.asarray(g, BF16), values, jnp.zeros((32, LANES), BF16)
+                )
         placed = jnp.dot(relay_left[...], slot_hot[...], preferred_element_type=F32)
         for g in range(TABLE):
             block = placed[g * 32 : (g + 1) * 32]
@@ -342,6 +344,10 @@
     for copy in info_trade:
         copy.start()
     push[...] = jnp.zeros_like(push)
+    zero16 = jnp.zeros((16, LANES), BF16)
+    for t in range(2 * TILES):
+        part = lax.shift_right_logical(pairs_ref[t : t + 1, :], 8).astype(F32)
+        block_of[t] = jnp.broadcast_to(part, (16, LANES)).astype(BF16)
     impulse[...] = jnp.zeros_like(impulse)
     geo[...] = jnp.ones_like(geo)
 
@@ -458,25 +464,36 @@
             push[1, lin] = (-const[24] * force[i])[0:TILES]
             push[0, ang] = (const[21 + i] * torque_a[i])[0:TILES]
             push[1, ang] = (-const[25 + i] * torque_b[i])[0:TILES]
+        lefts = []
         for e in range(2):
             for t in range(TILES):
                 value = push[e, pl.ds(t, 8, stride=TILES), :]
                 upper = coarse(value)
-                lower = value - upper
-                part = lax.shift_right_logical(index[e, t : t + 1], 8)
-                pieces = [
-                    jnp.where(part == h, half, 0.0) for half in (upper, lower) for h in range(3)
-                ]
-                at = (e * TILES + t) * LANES
-                push_left[:, at : at + LANES] = jnp.concatenate(pieces, axis=0).astype(BF16)
-        total = jnp.dot(push_left[...], pair_hot[...], preferred_element_type=F32)
+                both = jnp.concatenate([upper, value - upper], axis=0).astype(BF16)
+                lefts.append(
+                    jnp.concatenate(
+                        [
+                            jnp.where(block_of[e * TILES + t] == jnp.asarray(h, BF16), both, zero16)
+                            for h in range(2 + e)
+                        ],
+                        axis=0,
+                    )
+                )
+        def product(first, count):
+            return jnp.dot(
+                jnp.concatenate(lefts[first : first + count], axis=1),
+                pair_hot[first * LANES : (first + count) * LANES, :],
+                preferred_element_type=F32,
+            )
+
+        total_a = sum(product(f, CHUNK) for f in range(0, TILES, CHUNK))
+        total_b = sum(product(f, CHUNK) for f in range(TILES, 2 * TILES, CHUNK))
         for h in range(3):
             cols = slice(h * SPLIT, (h + 1) * SPLIT)
-            table[0:8, cols] = (
-                table[0:8, cols]
-                + total[h * 8 : (h + 1) * 8]
-                + total[24 + h * 8 : 32 + h * 8]
-            )
+            gain = total_b[h * 16 : h * 16 + 8] + total_b[h * 16 + 8 : h * 16 + 16]
+            if h < 2:
+                gain = gain + total_a[h * 16 : h * 16 + 8] + total_a[h * 16 + 8 : h * 16 + 16]
+            table[0:8, cols] = table[0:8, cols] + gain
         return carry
 
     for copy in info_trade:
@@ -594,7 +611,7 @@
             pltpu.VMEM((2 * TILES * LANES, SPLIT), BF16),
             pltpu.VMEM((32, TILES * LANES), F32),
             pltpu.VMEM((192, TILES * LANES), BF16),
-            pltpu.VMEM((48, 2 * TILES * LANES), BF16),
+            pltpu.VMEM((2 * TILES, 16, LANES), BF16),
             pltpu.VMEM((WIN, 10 * TILES, LANES), F32),
             pltpu.VMEM((WIN - 1, 10 * TILES, LANES), F32),
             pltpu.VMEM((10, ROWS, LANES), F32),

time: 37.9 us -> 37.5 us (0.989)
  Pallas kernels: 35.9 us -> 35.5 us
    pallas_call x1, Pallas kernels: 35.9 us -> 35.5 us  [on_device(): pl.pallas_call(lambda *refs: kernel(n_sub, n_layer, *refs), out_shape=(ja...]
where the time goes in v4:
time: 37.5 us; the launch traced here: 37.3 us
  Pallas kernels  35.5 us (95%)
  local copies, waits for them, and re-layouts  1.22 us (3%)
  between operations  0.64 us (2%)
    pallas_call x1, Pallas kernels, on_device(): pl.pallas_call(lambda *refs: kernel(n_sub, n_layer, *refs), out_shape=(ja...  35.5 us

profile of v4, /device:TPU:8, one launch (start us, length us, event | category | flops | bytes accessed | tf_op | source)
XLA Modules:
  0.0 37.3 jit_solution(10414323097247379434)
XLA Ops:
  0.6 35.5 %shard_map.86 = (f32[36,128]{1,0:T(8,128)S(1)}, f32[24,128]{1,0:T(8,128)S(1)}) custom-call(f32[120,128]{1,0:T(8,128)} %bitcast.7, s32[12,1,128]{2,1,0:T(1,128)} %bitcast.11, s32[24,128]{1,0:T(8,128)} %bitcast.8, s32[1,12]{1,0:T(1,128)} %refs_3_.1, f32[24,128]{1,0:T(8,128)} %bitcast.9, f32[16,128]{1,0:T(8,128)} %bitcast.10, s32[4,1,64]{2,1,0:T(1,128)} %refs_6_.1), custom_call_target="tpu_custom_call" | custom-call | tf_op jit(solution)/shard_map/pallas_call | solution.py:593
  36.1 0.6 %reshape.32 = f32[3,1,1536]{2,1,0:T(1,128)} reshape(f32[36,128]{1,0:T(8,128)S(1)} %get-tuple-element.4) | data formatting | bytes 36864 | tf_op jit(solution)/shard_map/reshape | solution.py:660
  36.7 0.6 %copy.14 = f32[6,1,512]{2,1,0:T(1,128)} copy(f32[6,1,512]{2,1,0:T(1,128)S(1)} %bitcast.6) | data formatting | bytes 24576

commit v5 on v4

--- a/solution.py
+++ b/solution.py
@@ -252,11 +252,6 @@
 
     upright_hot(slot_ref[...], slot_hot)
 
-    pl.semaphore_wait(barrier, 7)
-    first_trade = trade(0, lambda pair: first_out.at[pair], first_in)
-    for copy in first_trade:
-        copy.start()
-
     def relay_copy(step):
         return pltpu.make_async_remote_copy(
             src_ref=outgoing.at[lax.rem(place + step, WIN)],
@@ -289,14 +284,17 @@
                 outgoing[target, pl.ds(t, 8, stride=TILES), :] = main[:, cols]
                 outgoing[target, pl.ds(8 * TILES + t, 2, stride=TILES), :] = rest[:, cols]
 
-    def send_part(turn, carry):
-        swing = 1 - 2 * lax.rem(place, 2)
-        step = 2 + swing * lax.rem(turn, 2) - swing * (turn // 2)
+    def arrange_for(step, carry):
         arrange(lax.rem(place + step, WIN))
+        return carry
+
+    lax.fori_loop(1, WIN, arrange_for, 0)
+    pl.semaphore_wait(barrier, 7)
+    first_trade = trade(0, lambda pair: first_out.at[pair], first_in)
+    for copy in first_trade:
+        copy.start()
+    for step in (2, 1, 3):
         relay_copy(step).start()
-        return carry
-
-    lax.fori_loop(0, WIN - 1, send_part, 0)
     arrange(place)
 
     index[...] = jnp.zeros_like(index)

time: 37.5 us -> 36.5 us (0.973)
  Pallas kernels: 35.5 us -> 34.5 us
    pallas_call x1, Pallas kernels: 35.5 us -> 34.5 us  [on_device(): pl.pallas_call(lambda *refs: kernel(n_sub, n_layer, *refs), out_shape=(ja...]
where the time goes in v5:
time: 36.5 us; the launch traced here: 36.3 us
  Pallas kernels  34.5 us (95%)
  local copies, waits for them, and re-layouts  1.22 us (3%)
  between operations  0.64 us (2%)
    pallas_call x1, Pallas kernels, on_device(): pl.pallas_call(lambda *refs: kernel(n_sub, n_layer, *refs), out_shape=(ja...  34.5 us

profile of v5, /device:TPU:8, one launch (start us, length us, event | category | flops | bytes accessed | tf_op | source)
XLA Modules:
  0.0 36.3 jit_solution(1243856894328969819)
XLA Ops:
  0.6 34.5 %shard_map.86 = (f32[36,128]{1,0:T(8,128)S(1)}, f32[24,128]{1,0:T(8,128)S(1)}) custom-call(f32[120,128]{1,0:T(8,128)} %bitcast.7, s32[12,1,128]{2,1,0:T(1,128)} %bitcast.11, s32[24,128]{1,0:T(8,128)} %bitcast.8, s32[1,12]{1,0:T(1,128)} %refs_3_.1, f32[24,128]{1,0:T(8,128)} %bitcast.9, f32[16,128]{1,0:T(8,128)} %bitcast.10, s32[4,1,64]{2,1,0:T(1,128)} %refs_6_.1), custom_call_target="tpu_custom_call" | custom-call | tf_op jit(solution)/shard_map/pallas_call | solution.py:591
  35.1 0.6 %reshape.32 = f32[3,1,1536]{2,1,0:T(1,128)} reshape(f32[36,128]{1,0:T(8,128)S(1)} %get-tuple-element.4) | data formatting | bytes 36864 | tf_op jit(solution)/shard_map/reshape | solution.py:658
  35.7 0.6 %copy.14 = f32[6,1,512]{2,1,0:T(1,128)} copy(f32[6,1,512]{2,1,0:T(1,128)S(1)} %bitcast.6) | data formatting | bytes 24576

commit v6 on v5

--- a/solution.py
+++ b/solution.py
@@ -20,6 +20,7 @@
 friction = 0.6
 tangent_floor = 0.1
 
+NEAR = ((-1, 0), (1, 0), (0, -1), (0, 1))
 FAR = ((-2, 0), (2, 0), (0, -2), (0, 2), (-1, -1), (-1, 1), (1, -1), (1, 1))
 MESH = pl.DeviceIdType.MESH
 F32 = jnp.float32
@@ -115,34 +116,47 @@
     layer = lax.axis_index("layer")
     base = (sub // WIN) * WIN
     place = sub - base
-    lower_sub = lax.rem(sub + n_sub - 1, n_sub)
-    higher_sub = lax.rem(sub + 1, n_sub)
-    lower_layer = lax.rem(layer + n_layer - 1, n_layer)
-    higher_layer = lax.rem(layer + 1, n_layer)
-
     def mate(step):
         return base + lax.rem(place + step, WIN)
 
-    around = (
-        ((lower_sub, layer), 1, 0),
-        ((higher_sub, layer), 0, 0),
-        ((sub, lower_layer), 3, 1),
-        ((sub, higher_layer), 2, 1),
-    )
-
-    far = tuple(
-        (
-            (lax.rem(sub + n_sub + right, n_sub), lax.rem(layer + n_layer + up, n_layer)),
-            FAR.index((-right, -up)),
-            2 if right == 0 else 1,
-            1 if right == 0 or up == 0 else 2,
-        )
-        for right, up in FAR
-    )
+    def reach(right, up):
+        there, above = sub + right, layer + up
+        return (there >= 0) & (there < n_sub) & (above >= 0) & (above < n_layer)
+
+    def device(right, up):
+        return (
+            lax.rem(sub + n_sub + right, n_sub),
+            lax.rem(layer + n_layer + up, n_layer),
+        )
+
+    def start_all(copies):
+        for copy, right, up in copies:
+            pl.when(reach(right, up))(copy.start)
+
+    def take_all(copies):
+        for copy, right, up in copies:
+            pl.when(reach(-right, -up))(copy.wait_recv)
+
+    def sent_all(copies):
+        for copy, right, up in copies:
+            pl.when(reach(right, up))(copy.wait_send)
+
+    first_in[...] = jnp.zeros_like(first_in)
+    info_in[...] = jnp.zeros_like(info_in)
+    near_in[...] = jnp.zeros_like(near_in)
+    far_in[...] = jnp.zeros_like(far_in)
 
     barrier = pltpu.get_barrier_semaphore()
-    for device, _, _ in around:
-        pl.semaphore_signal(barrier, inc=1, device_id=device, device_id_type=MESH)
+    greeted = jnp.int32(WIN - 1)
+    for right, up in NEAR:
+
+        @pl.when(reach(right, up))
+        def _():
+            pl.semaphore_signal(
+                barrier, inc=1, device_id=device(right, up), device_id_type=MESH
+            )
+
+        greeted = greeted + reach(right, up).astype(jnp.int32)
     for step in range(1, WIN):
         pl.semaphore_signal(
             barrier, inc=1, device_id=(mate(step), layer), device_id_type=MESH
@@ -166,17 +180,19 @@
         load.start()
 
     def trade(step, source_of, dst):
-        return [
-            pltpu.make_async_remote_copy(
-                src_ref=source_of(pair),
+        copies = []
+        for right, up in NEAR:
+            slot = NEAR.index((-right, -up))
+            copy = pltpu.make_async_remote_copy(
+                src_ref=source_of(0 if up == 0 else 1),
                 dst_ref=dst.at[slot],
                 send_sem=near_send.at[step, slot],
                 recv_sem=near_recv.at[step, slot],
-                device_id=device,
+                device_id=device(right, up),
                 device_id_type=MESH,
             )
-            for device, slot, pair in around
-        ]
+            copies.append((copy, right, up))
+        return copies
 
     def near_copies(sweep):
         return trade(
@@ -184,17 +200,20 @@
         )
 
     def far_copies(sweep):
-        return [
-            pltpu.make_async_remote_copy(
+        copies = []
+        for right, up in FAR:
+            slot = FAR.index((-right, -up))
+            first, count = 2 if right == 0 else 1, 1 if right == 0 or up == 0 else 2
+            copy = pltpu.make_async_remote_copy(
                 src_ref=sweep_out.at[sweep, pl.ds(first, count)],
                 dst_ref=far_in.at[sweep, slot, pl.ds(0, count)],
                 send_sem=far_send.at[sweep, slot],
                 recv_sem=far_recv.at[sweep, slot],
-                device_id=device,
+                device_id=device(right, up),
                 device_id_type=MESH,
             )
-            for device, slot, first, count in far
-        ]
+            copies.append((copy, right, up))
+        return copies
 
     lane8 = lax.broadcasted_iota(jnp.int32, (8, LANES), 1)
     lane16 = lax.broadcasted_iota(jnp.int32, (ROWS, LANES), 1)
@@ -289,10 +308,9 @@
         return carry
 
     lax.fori_loop(1, WIN, arrange_for, 0)
-    pl.semaphore_wait(barrier, 7)
+    pl.semaphore_wait(barrier, greeted)
     first_trade = trade(0, lambda pair: first_out.at[pair], first_in)
-    for copy in first_trade:
-        copy.start()
+    start_all(first_trade)
     for step in (2, 1, 3):
         relay_copy(step).start()
     arrange(place)
@@ -339,8 +357,7 @@
     for pair in range(2):
         info_out[pair] = pick_listed(pair, 8, info)
     info_trade = trade(1, lambda pair: info_out.at[pair], info_in)
-    for copy in info_trade:
-        copy.start()
+    start_all(info_trade)
     push[...] = jnp.zeros_like(push)
     zero16 = jnp.zeros((16, LANES), BF16)
     for t in range(2 * TILES):
@@ -362,8 +379,7 @@
             ),
         )
 
-    for copy in first_trade:
-        copy.wait_recv()
+    take_all(first_trade)
     table[:, 512:640], table[:, 640:768] = halves(lane16, [first_in[slot] for slot in range(4)])
 
     def pick(component, e):
@@ -494,8 +510,7 @@
             table[0:8, cols] = table[0:8, cols] + gain
         return carry
 
-    for copy in info_trade:
-        copy.wait_recv()
+    take_all(info_trade)
     hints[0], hints[1] = halves(lane8, [info_in[slot] for slot in range(4)])
 
     def pull(row_block, pair, row):
@@ -512,16 +527,13 @@
 
         @pl.when(on)
         def _():
-            for copy in far_copies(sweep):
-                copy.start()
+            start_all(far_copies(sweep))
 
         for pair in range(2):
             sweep_out[sweep, 3 * pair] = pick_listed(pair, 8)
         near = near_copies(sweep)
-        for copy in near:
-            copy.start()
-        for copy in near:
-            copy.wait_recv()
+        start_all(near)
+        take_all(near)
         arrived = [
             jnp.where(lane8 < 64, near_in[sweep, 1, 1], near_in[sweep, 0, 1]),
             jnp.where(lane8 < 64, near_in[sweep, 3, 0], near_in[sweep, 2, 0]),
@@ -538,8 +550,7 @@
 
         @pl.when(on)
         def _():
-            for copy in far_copies(sweep):
-                copy.wait_recv()
+            take_all(far_copies(sweep))
 
             def landed(right, up, pair):
                 straight = right == 0 or up == 0
@@ -567,11 +578,9 @@
                         left, pull(side_a, pair, row), pull(side_b, pair, row)
                     )
                 table[0:8, copied[pair]] = was + total * hints[pair, 4:5]
-            for copy in far_copies(sweep):
-                copy.wait_send()
-
-        for copy in near:
-            copy.wait_send()
+            sent_all(far_copies(sweep))
+
+        sent_all(near)
         return carry
 
     lax.fori_loop(0, SWEEPS, one_sweep, 0)
@@ -579,8 +588,7 @@
         vel_out[pl.ds(h, 6, stride=OWN), :] = table[0:6, h * LANES : (h + 1) * LANES]
     for i in range(3):
         imp_out[i * TILES : (i + 1) * TILES, :] = impulse[i, 0:TILES]
-    for copy in first_trade + info_trade:
-        copy.wait_send()
+    sent_all(first_trade + info_trade)
     for step in range(1, WIN):
         relay_copy(step).wait_send()
 

time: 36.5 us -> 32.7 us (0.90)
  the two profiles are of different devices: /device:TPU:8 before, /device:TPU:6 now
where the time goes in v6:
time: 32.7 us; the launch traced here: 32.5 us
  Pallas kernels  30.7 us (94%)
  local copies, waits for them, and re-layouts  1.22 us (4%)
  between operations  0.64 us (2%)
    pallas_call x1, Pallas kernels, on_device(): pl.pallas_call(lambda *refs: kernel(n_sub, n_layer, *refs), out_shape=(ja...  30.7 us

profile of v6, /device:TPU:6, one launch (start us, length us, event | category | flops | bytes accessed | tf_op | source)
XLA Modules:
  0.0 32.5 jit_solution(9923116824220118622)
XLA Ops:
  0.6 30.7 %shard_map.86 = (f32[36,128]{1,0:T(8,128)S(1)}, f32[24,128]{1,0:T(8,128)S(1)}) custom-call(f32[120,128]{1,0:T(8,128)} %bitcast.7, s32[12,1,128]{2,1,0:T(1,128)} %bitcast.11, s32[24,128]{1,0:T(8,128)} %bitcast.8, s32[1,12]{1,0:T(1,128)} %refs_3_.1, f32[24,128]{1,0:T(8,128)} %bitcast.9, f32[16,128]{1,0:T(8,128)} %bitcast.10, s32[4,1,64]{2,1,0:T(1,128)} %refs_6_.1), custom_call_target="tpu_custom_call" | custom-call | tf_op jit(solution)/shard_map/pallas_call | solution.py:599
  31.3 0.6 %reshape.32 = f32[3,1,1536]{2,1,0:T(1,128)} reshape(f32[36,128]{1,0:T(8,128)S(1)} %get-tuple-element.4) | data formatting | bytes 36864 | tf_op jit(solution)/shard_map/reshape | solution.py:666
  31.9 0.6 %copy.14 = f32[6,1,512]{2,1,0:T(1,128)} copy(f32[6,1,512]{2,1,0:T(1,128)S(1)} %bitcast.6) | data formatting | bytes 24576

commit v7 on v6

--- a/solution.py
+++ b/solution.py
@@ -307,12 +307,18 @@
         arrange(lax.rem(place + step, WIN))
         return carry
 
-    lax.fori_loop(1, WIN, arrange_for, 0)
+    lax.fori_loop(1, 2, arrange_for, 0)
     pl.semaphore_wait(barrier, greeted)
     first_trade = trade(0, lambda pair: first_out.at[pair], first_in)
     start_all(first_trade)
-    for step in (2, 1, 3):
+    relay_copy(1).start()
+
+    def arrange_send(step, carry):
+        arrange(lax.rem(place + step, WIN))
         relay_copy(step).start()
+        return carry
+
+    lax.fori_loop(2, 4, arrange_send, 0)
     arrange(place)
 
     index[...] = jnp.zeros_like(index)

time: 32.7 us -> 32.3 us (0.988)
  Pallas kernels: 30.7 us -> 30.3 us
    pallas_call x1, Pallas kernels: 30.7 us -> 30.3 us  [on_device(): pl.pallas_call(lambda *refs: kernel(n_sub, n_layer, *refs), out_shape=(ja...]
where the time goes in v7:
time: 32.3 us; the launch traced here: 32.2 us
  Pallas kernels  30.3 us (94%)
  local copies, waits for them, and re-layouts  1.22 us (4%)
  between operations  0.64 us (2%)
    pallas_call x1, Pallas kernels, on_device(): pl.pallas_call(lambda *refs: kernel(n_sub, n_layer, *refs), out_shape=(ja...  30.3 us

profile of v7, /device:TPU:6, one launch (start us, length us, event | category | flops | bytes accessed | tf_op | source)
XLA Modules:
  0.0 32.2 jit_solution(3720781890460756957)
XLA Ops:
  0.6 30.3 %shard_map.86 = (f32[36,128]{1,0:T(8,128)S(1)}, f32[24,128]{1,0:T(8,128)S(1)}) custom-call(f32[120,128]{1,0:T(8,128)} %bitcast.7, s32[12,1,128]{2,1,0:T(1,128)} %bitcast.11, s32[24,128]{1,0:T(8,128)} %bitcast.8, s32[1,12]{1,0:T(1,128)} %refs_3_.1, f32[24,128]{1,0:T(8,128)} %bitcast.9, f32[16,128]{1,0:T(8,128)} %bitcast.10, s32[4,1,64]{2,1,0:T(1,128)} %refs_6_.1), custom_call_target="tpu_custom_call" | custom-call | tf_op jit(solution)/shard_map/pallas_call | solution.py:605
  30.9 0.6 %reshape.32 = f32[3,1,1536]{2,1,0:T(1,128)} reshape(f32[36,128]{1,0:T(8,128)S(1)} %get-tuple-element.4) | data formatting | bytes 36864 | tf_op jit(solution)/shard_map/reshape | solution.py:672
  31.6 0.6 %copy.14 = f32[6,1,512]{2,1,0:T(1,128)} copy(f32[6,1,512]{2,1,0:T(1,128)S(1)} %bitcast.6) | data formatting | bytes 24576

commit v8 on v7

--- a/solution.py
+++ b/solution.py
@@ -102,6 +102,7 @@
     info_out,
     info_in,
     hints,
+    far_spot,
     sweep_out,
     near_in,
     far_in,
@@ -307,18 +308,19 @@
         arrange(lax.rem(place + step, WIN))
         return carry
 
-    lax.fori_loop(1, 2, arrange_for, 0)
+    arrange_for(2, 0)
     pl.semaphore_wait(barrier, greeted)
     first_trade = trade(0, lambda pair: first_out.at[pair], first_in)
     start_all(first_trade)
-    relay_copy(1).start()
-
-    def arrange_send(step, carry):
+    relay_copy(2).start()
+
+    def arrange_send(turn, carry):
+        step = 1 + 2 * turn
         arrange(lax.rem(place + step, WIN))
         relay_copy(step).start()
         return carry
 
-    lax.fori_loop(2, 4, arrange_send, 0)
+    lax.fori_loop(0, 2, arrange_send, 0)
     arrange(place)
 
     index[...] = jnp.zeros_like(index)
@@ -516,11 +518,8 @@
             table[0:8, cols] = table[0:8, cols] + gain
         return carry
 
-    take_all(info_trade)
-    hints[0], hints[1] = halves(lane8, [info_in[slot] for slot in range(4)])
-
     def pull(row_block, pair, row):
-        spot = jnp.broadcast_to(hints[pair, row : row + 1], (8, LANES)).astype(jnp.int32)
+        spot = far_spot[pair * 4 + row]
         return jnp.where(spot >= 0, take(row_block, jnp.maximum(spot, 0)), 0.0)
 
     def one_sweep(sweep, carry):
@@ -539,6 +538,24 @@
             sweep_out[sweep, 3 * pair] = pick_listed(pair, 8)
         near = near_copies(sweep)
         start_all(near)
+
+        @pl.when(sweep == 0)
+        def _():
+            take_all(info_trade)
+            hints[0], hints[1] = halves(lane8, [info_in[slot] for slot in range(4)])
+            for pair in range(2):
+                for row in range(4):
+                    far_spot[pair * 4 + row] = jnp.broadcast_to(
+                        hints[pair, row : row + 1], (8, LANES)
+                    ).astype(jnp.int32)
+            sent_all(first_trade + info_trade)
+            for step in range(1, WIN):
+                relay_copy(step).wait_send()
+
+        @pl.when(sweep > 0)
+        def _():
+            sent_all(near_copies(sweep - 1) + far_copies(sweep - 1))
+
         take_all(near)
         arrived = [
             jnp.where(lane8 < 64, near_in[sweep, 1, 1], near_in[sweep, 0, 1]),
@@ -584,9 +601,7 @@
                         left, pull(side_a, pair, row), pull(side_b, pair, row)
                     )
                 table[0:8, copied[pair]] = was + total * hints[pair, 4:5]
-            sent_all(far_copies(sweep))
-
-        sent_all(near)
+
         return carry
 
     lax.fori_loop(0, SWEEPS, one_sweep, 0)
@@ -594,9 +609,7 @@
         vel_out[pl.ds(h, 6, stride=OWN), :] = table[0:6, h * LANES : (h + 1) * LANES]
     for i in range(3):
         imp_out[i * TILES : (i + 1) * TILES, :] = impulse[i, 0:TILES]
-    sent_all(first_trade + info_trade)
-    for step in range(1, WIN):
-        relay_copy(step).wait_send()
+    sent_all(near_copies(SWEEPS - 1))
 
 
 def on_device(n_sub, n_layer, geometry, dest_slot, pairs, colors, free_vel, inertia, exports):
@@ -642,6 +655,7 @@
             pltpu.VMEM((2, 8, LANES), F32),
             pltpu.VMEM((4, 8, LANES), F32),
             pltpu.VMEM((2, 8, LANES), F32),
+            pltpu.VMEM((8, 8, LANES), jnp.int32),
             pltpu.VMEM((SWEEPS, 4, 8, LANES), F32),
             pltpu.VMEM((SWEEPS, 4, 2, 8, LANES), F32),
             pltpu.VMEM((SWEEPS - 1, 8, 2, 8, LANES), F32),

time: 32.3 us -> 32 us (level)
  no operation moved by 1% of the time
where the time goes in v8:
time: 32 us; the launch traced here: 31.9 us
  Pallas kernels  30 us (94%)
  local copies, waits for them, and re-layouts  1.22 us (4%)
  between operations  0.64 us (2%)
    pallas_call x1, Pallas kernels, on_device(): pl.pallas_call(lambda *refs: kernel(n_sub, n_layer, *refs), out_shape=(ja...  30 us

profile of v8, /device:TPU:6, one launch (start us, length us, event | category | flops | bytes accessed | tf_op | source)
XLA Modules:
  0.0 31.9 jit_solution(16456394112594531058)
XLA Ops:
  0.6 30.0 %shard_map.86 = (f32[36,128]{1,0:T(8,128)S(1)}, f32[24,128]{1,0:T(8,128)S(1)}) custom-call(f32[120,128]{1,0:T(8,128)} %bitcast.7, s32[12,1,128]{2,1,0:T(1,128)} %bitcast.11, s32[24,128]{1,0:T(8,128)} %bitcast.8, s32[1,12]{1,0:T(1,128)} %refs_3_.1, f32[24,128]{1,0:T(8,128)} %bitcast.9, f32[16,128]{1,0:T(8,128)} %bitcast.10, s32[4,1,64]{2,1,0:T(1,128)} %refs_6_.1), custom_call_target="tpu_custom_call" | custom-call | tf_op jit(solution)/shard_map/pallas_call | solution.py:618
  30.7 0.6 %reshape.32 = f32[3,1,1536]{2,1,0:T(1,128)} reshape(f32[36,128]{1,0:T(8,128)S(1)} %get-tuple-element.4) | data formatting | bytes 36864 | tf_op jit(solution)/shard_map/reshape | solution.py:686
  31.3 0.6 %copy.14 = f32[6,1,512]{2,1,0:T(1,128)} copy(f32[6,1,512]{2,1,0:T(1,128)S(1)} %bitcast.6) | data formatting | bytes 24576
